TPU v7x, 32 devices: a whole 2x2x4 slice. The times are simulated.
32 devices in a mesh: groups: 1, pool: 2 (over core), dev: 16 (over z, y, x).
Axes of the slice: x: 2, y: 2, z: 4, core: 2. Of those that a mesh axis runs over, the one named last changes fastest.
Arguments:
- residual_in: bfloat16 [256, 4096], P(('groups', 'pool', 'dev')), may hold values from -6 to 6
- queries: bfloat16 [256, 8192], P(('groups', 'pool', 'dev')), may hold values from -120 to 120
- key_cache: bfloat16 [256, 128, 512], P(('groups', 'pool', 'dev')), may hold values from -4.5 to 4.5
- value_cache: bfloat16 [256, 128, 512], P(('groups', 'pool', 'dev')), may hold values from -6 to 6
- new_keys: bfloat16 [256, 512], P(('groups', 'pool', 'dev')), may hold values from -4 to 4
- new_values: bfloat16 [256, 512], P(('groups', 'pool', 'dev')), may hold values from -6 to 6
- lengths: int32 [256], P(('groups', 'pool', 'dev')), may hold values from 1 to 128, 16384 in all
- out_weight: bfloat16 [8192, 4096], P('dev'), may hold values from -0.5 to 0.5
- norm_gain: bfloat16 [4096], replicated, may hold values from 0.5 to 1.5
- expert_ids: int32 [256, 8], P(('groups', 'pool', 'dev')), may hold values from 0 to 15, all different within a row; in each aligned block of 8 rows (0 to 7, 8 to 15, ...) at most 4 rows name the same one
- route_weights: float32 [256, 8], P(('groups', 'pool', 'dev')), may hold values from 0.05 to 0.3
- w_gate: bfloat16 [16, 4096, 768], P('dev', None, 'pool'), may hold values from -0.09375 to 0.09375
- w_up: bfloat16 [16, 4096, 768], P('dev', None, 'pool'), may hold values from -0.09375 to 0.09375
- w_down: bfloat16 [16, 768, 4096], P('dev', 'pool'), may hold values from -0.21875 to 0.21875
Outputs:
- layer_out: bfloat16 [256, 4096], P(('groups', 'pool', 'dev'))
Inputs may be any that keep to these rules, and one draw needn't show every extreme that they name: `expert_ids`: each row names 8 different experts; within the 8 rows of one device no expert is named more than 4 times, a bound that some block reaches.
All inputs are finite; a program needn't handle non-finite values. No bound on the sum of `lengths` on one device may be relied on, other than what follows from the above.
Results may differ from a plain program's by a relative error of at most 0.008.
Values may be sent and summed in bfloat16 or wider, within the bound.
A program may use at most 64 MiB of HBM per device.

v0:
```python
import math

import jax
import jax.numpy as jnp
from jax import lax
from jax.sharding import PartitionSpec as P

H = 64
KVH = 4
HD = 128
TOPK = 8


def attend(queries, key_cache, value_cache, new_keys, new_values, lengths):
    rows = queries.shape[0]
    span = key_cache.shape[1]
    group = H // KVH
    query_heads = queries.reshape(rows, KVH, group, HD)
    keys_all = key_cache.reshape(rows, span, KVH, HD)
    values_all = value_cache.reshape(rows, span, KVH, HD)
    scale = 1.0 / math.sqrt(HD)
    scores = (
        jnp.einsum("rkgd,rlkd->rkgl", query_heads, keys_all, preferred_element_type=jnp.float32)
        * scale
    )
    own = (
        jnp.einsum(
            "rkgd,rkd->rkg",
            query_heads,
            new_keys.reshape(rows, KVH, HD),
            preferred_element_type=jnp.float32,
        )
        * scale
    )
    valid = (jnp.arange(span, dtype=jnp.int32)[None, :] < lengths[:, None])[:, None, None, :]
    scores = jnp.where(valid, scores, -1e30)
    top = jnp.maximum(jnp.max(scores, axis=-1), own)
    weights = jnp.where(valid, jnp.exp(scores - top[..., None]), 0.0)
    own_weight = jnp.exp(own - top)
    total = jnp.sum(weights, axis=-1) + own_weight
    weights = (weights / total[..., None]).astype(jnp.bfloat16)
    own_weight = (own_weight / total).astype(jnp.bfloat16)
    mixed = jnp.einsum("rkgl,rlkd->rkgd", weights, values_all, preferred_element_type=jnp.float32)
    mixed = mixed + own_weight.astype(jnp.float32)[..., None] * new_values.reshape(
        rows, KVH, 1, HD
    ).astype(jnp.float32)
    return mixed.reshape(rows, H * HD).astype(jnp.bfloat16)


def local(
    residual_in,
    queries,
    key_cache,
    value_cache,
    new_keys,
    new_values,
    lengths,
    out_weight,
    norm_gain,
    expert_ids,
    route_weights,
    w_gate,
    w_up,
    w_down,
):
    rows = residual_in.shape[0]
    heads_out = attend(queries, key_cache, value_cache, new_keys, new_values, lengths)
    regrouped = lax.all_to_all(heads_out, "dev", split_axis=1, concat_axis=0, tiled=True)
    attn_out = lax.psum_scatter(
        jnp.dot(regrouped, out_weight, preferred_element_type=jnp.float32),
        "dev",
        scatter_dimension=0,
        tiled=True,
    )
    hidden = residual_in.astype(jnp.float32) + attn_out
    mean_square = jnp.mean(hidden * hidden, axis=-1, keepdims=True)
    normed = (hidden * lax.rsqrt(mean_square + 1e-06) * norm_gain.astype(jnp.float32)).astype(
        jnp.bfloat16
    )
    experts = lax.axis_size("dev")
    slots_per = max(2, (rows * TOPK + experts - 1) // experts)
    flat_ids = expert_ids.reshape(rows * TOPK)
    onehot = (flat_ids[:, None] == jnp.arange(experts, dtype=jnp.int32)[None, :]).astype(jnp.int32)
    slot = jnp.sum((jnp.cumsum(onehot, axis=0) - 1) * onehot, axis=1)
    pick_expert = onehot.astype(jnp.float32).reshape(rows, TOPK, experts)
    pick_slot = (
        (slot[:, None] == jnp.arange(slots_per, dtype=jnp.int32)[None, :])
        .astype(jnp.float32)
        .reshape(rows, TOPK, slots_per)
    )
    dispatch = (
        jnp.einsum("rke,rkc->ecr", pick_expert, pick_slot)
        .reshape(experts * slots_per, rows)
        .astype(jnp.bfloat16)
    )
    outgoing = jnp.dot(dispatch, normed, preferred_element_type=jnp.float32).astype(jnp.bfloat16)
    combine = jnp.einsum("rk,rke,rkc->rec", route_weights, pick_expert, pick_slot).reshape(
        rows, experts * slots_per
    )
    arrived = lax.all_to_all(outgoing, "dev", split_axis=0, concat_axis=0, tiled=True)
    block = lax.all_gather(arrived, "pool", axis=0, tiled=True)
    gate_proj = jnp.dot(block, w_gate[0], preferred_element_type=jnp.float32)
    up_proj = jnp.dot(block, w_up[0], preferred_element_type=jnp.float32)
    activated = (jax.nn.silu(gate_proj) * up_proj).astype(jnp.bfloat16)
    partial_value = jnp.dot(activated, w_down[0], preferred_element_type=jnp.float32)
    summed = lax.psum_scatter(
        partial_value.astype(jnp.bfloat16), "pool", scatter_dimension=0, tiled=True
    )
    returned = lax.all_to_all(summed, "dev", split_axis=0, concat_axis=0, tiled=True)
    moe = jnp.dot(combine, returned.astype(jnp.float32), precision=lax.Precision.HIGHEST)
    return (hidden + moe).astype(jnp.bfloat16)


def solution(mesh):
    placed = (
        P(("groups", "pool", "dev"), None),
        P(("groups", "pool", "dev"), None),
        P(("groups", "pool", "dev"), None, None),
        P(("groups", "pool", "dev"), None, None),
        P(("groups", "pool", "dev"), None),
        P(("groups", "pool", "dev"), None),
        P(("groups", "pool", "dev")),
        P("dev", None),
        P(),
        P(("groups", "pool", "dev"), None),
        P(("groups", "pool", "dev"), None),
        P("dev", None, "pool"),
        P("dev", None, "pool"),
        P("dev", "pool", None),
    )
    return jax.shard_map(
        local,
        mesh=mesh,
        in_specs=placed,
        out_specs=P(("groups", "pool", "dev"), None),
        check_vma=False,
    )
```

profile of v0, /device:TPU:0, one launch (start us, length us, event | category | flops | bytes accessed | tf_op | source)
XLA Modules:
  0.0 192.1 jit_solution(9578284820436262395)
XLA Ops:
  6.5 0.9 iota_compare_fusion.7
  7.4 1.2 fusion.35
  8.6 2.0 %fusion.61 = (f32[8,4,16]{2,1,0:T(4,128)S(1)}, f32[8,4,16,128]{3,2,1,0:T(8,128)S(1)}) fusion(bf16[8,4,16,128]{3,0,2,1:T(8,128)(2,1)} %bitcast.61, pred[8,128]{1,0:T(8,128)(4,1)S(1)} %iota_compare_fusion.7, bf16[8,128,512]{2,1,0:T(8,128)(2,1)} %param.16), kind=kOutput, calls=%fused_computation.76 | convolution fusion | flops 16973312 | bytes 1444864 | tf_op jit(solution)/shard_map/rkgd,rlkd->rkgl/dot_general | solution.py:23
  10.6 0.3 fusion.23
  11.0 0.7 bitcast_convert_fusion
  11.7 1.7 fusion.8
  13.5 15.9 %all_to_all.37 = bf16[8,16,512]{2,0,1:T(8,128)(2,1)S(1)} all-to-all(bf16[8,16,512]{2,0,1:T(8,128)(2,1)S(1)} %copy.31), channel_id=1, replica_groups=mesh['groups'=1,'pool'=2,'dev'=16] {'dev'}, dimensions={1} | all-to-all | bytes 262144 | tf_op jit(solution)/shard_map/all_to_all | solution.py:68
  29.5 4.3 %fusion.29 = f32[128,4096]{1,0:T(8,128)} fusion(bf16[512,4096]{1,0:T(8,128)(2,1)} %param.21, bf16[8,16,512]{2,0,1:T(8,128)(2,1)S(1)} %all_to_all.37), kind=kOutput, calls=%fused_computation.31 | convolution fusion | flops 536870912 | bytes 6422528 | tf_op jit(solution)/shard_map/dot_general | solution.py:70
  34.4 0.2 fusion.15
  34.7 76.9 %reduce-scatter.3.cloned.1.call-done = f32[8,4096]{1,0:T(8,128)} async-done(((f32[128,4096]{1,0:T(8,128)}), f32[8,4096]{1,0:T(8,128)}) %reduce-scatter.3.cloned.1.call-update) | async-done | bytes 131088 | tf_op jit(solution)/shard_map/reduce_scatter | solution.py:69
  111.6 1.1 multiply_reduce_fusion
  112.7 2.1 %convolution_convert_fusion.1 = bf16[64,4096]{1,0:T(8,128)(2,1)} fusion(bf16[64,8]{1,0:T(8,128)(2,1)S(1)} %bitcast.64, f32[4096]{0:T(1024)S(1)} %convert_element_type.83, f32[8]{0:T(128)S(1)} %add_rsqrt_fusion, f32[8,4096]{1,0:T(8,128)} %reduce-scatter.3.cloned.1.call-done, bf16[8,4096]{1,0:T(8,128)(2,1)S(1)} %copy-done.2), kind=kOutput, calls=%fused_computation.1 | convolution fusion | flops 4620288 | bytes 738336 | tf_op jit(solution)/shard_map/dot_general | solution.py:96
  114.7 2.0 %all_to_all.29 = bf16[16,4,4096]{2,1,0:T(4,128)(2,1)} reshape(bf16[64,4096]{1,0:T(8,128)(2,1)} %convolution_convert_fusion.1) | data formatting | bytes 1048576 | tf_op jit(solution)/shard_map/all_to_all | solution.py:100
  116.8 15.0 %all_to_all.38 = bf16[16,4,4096]{2,1,0:T(4,128)(2,1)} all-to-all(bf16[16,4,4096]{2,1,0:T(4,128)(2,1)} %all_to_all.29), channel_id=1, replica_groups=mesh['groups'=1,'pool'=2,'dev'=16] {'dev'}, dimensions={0} | all-to-all | bytes 1048576 | tf_op jit(solution)/shard_map/all_to_all | solution.py:100
  131.8 2.0 %all_to_all.31 = bf16[64,4096]{1,0:T(8,128)(2,1)} reshape(bf16[16,4,4096]{2,1,0:T(4,128)(2,1)} %all_to_all.38) | data formatting | bytes 1048576 | tf_op jit(solution)/shard_map/all_to_all | solution.py:100
  133.8 7.5 %all-gather.2.cloned.1.call-done = bf16[128,4096]{1,0:T(8,128)(2,1)} async-done(((bf16[64,4096]{1,0:T(8,128)(2,1)}), bf16[128,4096]{1,0:T(8,128)(2,1)}) %all-gather.2.cloned.1.call-update) | async-done | bytes 1048592 | tf_op jit(solution)/shard_map/all_gather | solution.py:101
  141.3 2.9 %fusion.5 = f32[128,384]{1,0:T(8,128)S(1)} fusion(bf16[128,4096]{1,0:T(8,128)(2,1)} %all-gather.2.cloned.1.call-done, bf16[1,4096,384]{2,1,0:T(8,128)(2,1)} %param.25), kind=kOutput, calls=%fused_computation.8 | convolution fusion | flops 402653184 | bytes 4390912 | tf_op jit(solution)/shard_map/dot_general | solution.py:102
  144.3 4.6 %convolution_convert_fusion = bf16[128,4096]{1,0:T(8,128)(2,1)} fusion(bf16[1,384,4096]{2,1,0:T(8,128)(2,1)S(1)} %copy-done, bf16[128,4096]{1,0:T(8,128)(2,1)} %all-gather.2.cloned.1.call-done, bf16[1,4096,384]{2,1,0:T(8,128)(2,1)} %param.26, f32[128,384]{1,0:T(8,128)S(1)} %fusion.5), kind=kOutput, calls=%fused_computation | convolution fusion | flops 806125568 | bytes 8585216 | tf_op jit(solution)/shard_map/dot_general | solution.py:105
  148.9 9.9 %reduce-scatter.5.cloned.1.call-done = bf16[64,4096]{1,0:T(8,128)(2,1)} async-done(((bf16[128,4096]{1,0:T(8,128)(2,1)}), bf16[64,4096]{1,0:T(8,128)(2,1)}) %reduce-scatter.5.cloned.1.call-update) | async-done | bytes 524304 | tf_op jit(solution)/shard_map/reduce_scatter | solution.py:106
  158.8 2.0 %all_to_all.32 = bf16[16,4,4096]{2,1,0:T(4,128)(2,1)} reshape(bf16[64,4096]{1,0:T(8,128)(2,1)} %reduce-scatter.5.cloned.1.call-done) | data formatting | bytes 1048576 | tf_op jit(solution)/shard_map/all_to_all | solution.py:109
  160.8 6.8 %all-to-all-start.2 = ((bf16[16,4,4096]{2,1,0:T(4,128)(2,1)}), bf16[16,4,4096]{2,1,0:T(4,128)(2,1)}, u32[]{:S(2)}, u32[]{:S(2)}) async-start(bf16[16,4,4096]{2,1,0:T(4,128)(2,1)} %all_to_all.32), calls=%async_computation.4 | async-start | bytes 1048576 | tf_op jit(solution)/shard_map/all_to_all | solution.py:109
  167.7 0.2 fusion.43
  167.9 15.3 %all-to-all-done.2 = bf16[16,4,4096]{2,1,0:T(4,128)(2,1)} async-done(((bf16[16,4,4096]{2,1,0:T(4,128)(2,1)}), bf16[16,4,4096]{2,1,0:T(4,128)(2,1)}, u32[]{:S(2)}, u32[]{:S(2)}) %all-to-all-start.2) | async-done | bytes 524320 | tf_op jit(solution)/shard_map/all_to_all | solution.py:109
  183.2 2.4 %fusion.1 = bf16[8,4096]{1,0:T(8,128)(2,1)} fusion(bf16[16,4,4096]{2,1,0:T(4,128)(2,1)} %all-to-all-done.2, f32[8,4096]{1,0:T(8,128)S(1)} %copy-done.1, bf16[8,4096]{1,0:T(8,128)(2,1)S(1)} %copy-done.2, f32[8,16,4]{1,2,0:T(4,128)S(1)} %fusion.43), kind=kOutput, calls=%fused_computation.4 | convolution fusion | flops 25296896 | bytes 788480 | tf_op jit(solution)/shard_map/dot_general | solution.py:110
  (31 shorter events, 1.0 us)
Async XLA Ops:
  6.5 137.7 %copy-start = (bf16[1,384,4096]{2,1,0:T(8,128)(2,1)S(1)}, bf16[1,384,4096]{2,1,0:T(8,128)(2,1)}, u32[]{:S(2)}) copy-start(bf16[1,384,4096]{2,1,0:T(8,128)(2,1)} %param.27) | copy-start | bytes 9437188
  6.5 105.1 %reduce-scatter.3.cloned.1.call-start = ((), (), s32[]{:S(2)}) async-start(), calls=%async_computation.5 | async-start | bytes 2228224 | tf_op jit(solution)/shard_map/reduce_scatter | solution.py:69
  29.4 4.4 %copy-start.4 = (s32[8,8]{1,0:T(8,128)S(1)}, s32[8,8]{1,0:T(8,128)}, u32[]{:S(2)}) copy-start(s32[8,8]{1,0:T(8,128)} %param.23) | copy-start | bytes 772
  29.4 5.3 %copy-start.3 = (bf16[4096]{0:T(1024)(128)(2,1)S(1)}, bf16[4096]{0:T(1024)(128)(2,1)}, u32[]{:S(2)}) copy-start(bf16[4096]{0:T(1024)(128)(2,1)} %param.22) | copy-start | bytes 24580
  29.5 82.2 %copy-start.2 = (bf16[8,4096]{1,0:T(8,128)(2,1)S(1)}, bf16[8,4096]{1,0:T(8,128)(2,1)}, u32[]{:S(2)}) copy-start(bf16[8,4096]{1,0:T(8,128)(2,1)} %param.14) | copy-start | bytes 196612
  33.8 107.5 %all-gather.2.cloned.1.call-start = ((), (), s32[]{:S(2)}) async-start(), calls=%async_computation.6 | async-start | bytes 1572864 | tf_op jit(solution)/shard_map/all_gather | solution.py:101
  133.8 25.0 %reduce-scatter.5.cloned.1.call-start = ((), (), s32[]{:S(2)}) async-start(), calls=%async_computation.7 | async-start | bytes 1572864 | tf_op jit(solution)/shard_map/reduce_scatter | solution.py:106
  148.9 18.8 %copy-start.5 = (f32[8,8]{1,0:T(8,128)S(1)}, f32[8,8]{1,0:T(8,128)}, u32[]{:S(2)}) copy-start(f32[8,8]{1,0:T(8,128)} %param.24) | copy-start | bytes 772
  148.9 34.3 %copy-start.1 = (f32[8,4096]{1,0:T(8,128)S(1)}, f32[8,4096]{1,0:T(8,128)}, u32[]{:S(2)}) copy-start(f32[8,4096]{1,0:T(8,128)} %reduce-scatter.3.cloned.1.call-done) | copy-start | bytes 393220
  160.8 22.3 %all-to-all-start.2 = ((bf16[16,4,4096]{2,1,0:T(4,128)(2,1)}), bf16[16,4,4096]{2,1,0:T(4,128)(2,1)}, u32[]{:S(2)}, u32[]{:S(2)}) async-start(bf16[16,4,4096]{2,1,0:T(4,128)(2,1)} %all_to_all.32), calls=%async_computation.4 | async-start | bytes 1048576 | tf_op jit(solution)/shard_map/all_to_all | solution.py:109
Sparse Core Ops, SparseCore 0:
  33.9 77.6 reduce-scatter.2
  133.9 7.4 all-gather.1
  149.1 9.6 reduce-scatter.4
where the time goes:
time: 193 us; the launch traced here: 192 us
  waiting for transfers between devices  110 us (57%)
  blocking collectives  30.9 us (16%)
  matrix products  21.7 us (11%)
  between operations  13.2 us (7%)
  starting transfers between devices  6.89 us (4%)
  local copies, waits for them, and re-layouts  6.51 us (3%)
  other arithmetic  3.32 us (2%)
    reduce_scatter x1, waiting for transfers between devices, local(): lax.psum_scatter(jnp.dot(regrouped, out_weight, preferred_element_type=jn...  76.9 us
    all_to_all x1, blocking collectives, local(): lax.all_to_all(heads_out, 'dev', split_axis=1, concat_axis=0, tiled=True)  15.9 us
    all_to_all x1, waiting for transfers between devices, local(): lax.all_to_all(summed, 'dev', split_axis=0, concat_axis=0, tiled=True)  15.3 us
    all_to_all x1, blocking collectives, local(): lax.all_to_all(outgoing, 'dev', split_axis=0, concat_axis=0, tiled=True)  15 us
    reduce_scatter x1, waiting for transfers between devices, local(): lax.psum_scatter(partial_value.astype(jnp.bfloat16), 'pool', scatter_dime...  9.86 us
    all_gather x1, waiting for transfers between devices, local(): block = lax.all_gather(arrived, 'pool', axis=0, tiled=True)  7.53 us
    all_to_all x1, starting transfers between devices, local(): lax.all_to_all(summed, 'dev', split_axis=0, concat_axis=0, tiled=True)  6.81 us
    dot_general x1, matrix products, local(): jnp.dot(activated, w_down[0], preferred_element_type=jnp.float32)  4.63 us
  transfers between devices with their start and end apart: 4, of which 4 were waited for; matrix products, arithmetic and copies ran while one was open for 1% of the time, Pallas kernels for 0%

commit v1 on v0

v1 whole, which is shorter than its diff:
```python
import functools
import math

import jax
import jax.numpy as jnp
from jax import lax
from jax.experimental import pallas as pl
from jax.experimental.pallas import tpu as pltpu
from jax.sharding import PartitionSpec as P

H = 64
KVH = 4
HD = 128
TOPK = 8


def attend(queries, key_cache, value_cache, new_keys, new_values, lengths):
    rows = queries.shape[0]
    span = key_cache.shape[1]
    group = H // KVH
    query_heads = queries.reshape(rows, KVH, group, HD)
    keys_all = key_cache.reshape(rows, span, KVH, HD)
    values_all = value_cache.reshape(rows, span, KVH, HD)
    scale = 1.0 / math.sqrt(HD)
    scores = (
        jnp.einsum("rkgd,rlkd->rkgl", query_heads, keys_all, preferred_element_type=jnp.float32)
        * scale
    )
    own = (
        jnp.einsum(
            "rkgd,rkd->rkg",
            query_heads,
            new_keys.reshape(rows, KVH, HD),
            preferred_element_type=jnp.float32,
        )
        * scale
    )
    valid = (jnp.arange(span, dtype=jnp.int32)[None, :] < lengths[:, None])[:, None, None, :]
    scores = jnp.where(valid, scores, -1e30)
    top = jnp.maximum(jnp.max(scores, axis=-1), own)
    weights = jnp.where(valid, jnp.exp(scores - top[..., None]), 0.0)
    own_weight = jnp.exp(own - top)
    total = jnp.sum(weights, axis=-1) + own_weight
    weights = (weights / total[..., None]).astype(jnp.bfloat16)
    own_weight = (own_weight / total).astype(jnp.bfloat16)
    mixed = jnp.einsum("rkgl,rlkd->rkgd", weights, values_all, preferred_element_type=jnp.float32)
    mixed = mixed + own_weight.astype(jnp.float32)[..., None] * new_values.reshape(
        rows, KVH, 1, HD
    ).astype(jnp.float32)
    return mixed.reshape(rows, H * HD).astype(jnp.bfloat16)


F32 = jnp.float32
BF16 = jnp.bfloat16
ROW = 16


def flip(index, mask):
    for bit in range(mask.bit_length()):
        if (mask >> bit) & 1:
            index = index + (1 << bit) * (1 - 2 * ((index // (1 << bit)) % 2))
    return index


def reverse_bits(value, bits):
    return sum(((value >> bit) & 1) << (bits - 1 - bit) for bit in range(bits))


def layer_kernel(n, *refs):
    bits = n.bit_length() - 1
    tails = bits - 2
    refs = list(refs)

    def take(count):
        taken = refs[:count]
        del refs[:count]
        return taken

    heads, residual, gain, wo_hbm, wg_hbm, wu_hbm, wd_hbm, out = take(8)
    hb, wo, wg, wu, wd, acc, gathered, other, pool_send, pool_recv = take(10)
    res_send, res_recv, sq_send, sq_recv, out_send, out_recv = take(6)
    s1a, s1b, r1a, r1b, s2a, s2b, r2a, r2b = take(8)
    tail_send, tail_recv = take(tails), take(tails)
    local_sem, heads_ss, heads_rs, pool_ss, pool_rs, rs_ss, rs_rs, ag_ss, ag_rs = take(9)

    me = lax.axis_index("dev")
    pool = lax.axis_index("pool")
    mate = {"pool": 1 - pool}
    first = pool == 0
    half = acc.shape[-1]
    quarter = half // 2
    width = wo.shape[0]
    fold = width // 2
    rows = n * ROW

    def remote(source, target, send_sem, recv_sem, device):
        return pltpu.make_async_remote_copy(
            src_ref=source,
            dst_ref=target,
            send_sem=send_sem,
            recv_sem=recv_sem,
            device_id=device,
            device_id_type=pl.DeviceIdType.MESH,
        )

    mine = pl.ds(pl.multiple_of(pool * half, half), half)
    theirs = pl.ds(pl.multiple_of((1 - pool) * half, half), half)
    loads = [
        (wo_hbm.at[:, mine], wo),
        (wg_hbm.at[0, mine], wg.at[0]),
        (wg_hbm.at[0, theirs], wg.at[1]),
        (wu_hbm.at[0, mine], wu.at[0]),
        (wu_hbm.at[0, theirs], wu.at[1]),
        (wd_hbm.at[0, :, mine], wd.at[0]),
        (wd_hbm.at[0, :, theirs], wd.at[1]),
        (heads.at[me], hb.at[pool, 0]),
    ]
    loads = [
        pltpu.make_async_copy(source, target, local_sem.at[i])
        for i, (source, target) in enumerate(loads)
    ]
    for load in (loads[7], loads[0]):
        load.start()

    barrier = pltpu.get_barrier_semaphore()
    pl.semaphore_signal(barrier, inc=1, device_id=mate, device_id_type=pl.DeviceIdType.MESH)
    for j in range(1, n):
        pl.semaphore_signal(
            barrier, inc=1, device_id={"dev": flip(me, j)}, device_id_type=pl.DeviceIdType.MESH
        )
    pl.semaphore_wait(barrier, n)

    sends = []
    for j in range(1, n):
        peer = flip(me, j)
        sends.append(
            remote(
                heads.at[peer],
                hb.at[pool, reverse_bits(j, bits)],
                heads_ss.at[j],
                heads_rs.at[j],
                {"dev": peer},
            )
        )
        sends[-1].start()
    for load in loads[1:7]:
        load.start()

    res = residual[...].astype(F32)
    res_own = jnp.where(first, res[:, :half], res[:, half:])
    res_send[...] = jnp.where(first, res[:, half:], res[:, :half])
    swap_res = remote(res_send, res_recv, pool_ss.at[0], pool_rs.at[0], mate)
    swap_res.start()

    loads[7].wait()
    for send in sends:
        send.wait_recv()
    forward = remote(hb.at[pool], hb.at[pool], pool_ss.at[1], pool_rs.at[1], mate)
    forward.start()
    for send in sends:
        send.wait_send()
    loads[0].wait()
    forward.wait()

    wide = hb[...].astype(F32)
    pairs = jnp.concatenate([wide[0, :, :8], wide[1, :, :8]], axis=1).reshape(rows, -1)
    lower = jnp.concatenate([wide[0, :, 8:], wide[1, :, 8:]], axis=1).reshape(rows, -1)
    left = pairs[:, :fold].astype(BF16)
    right = lower[:, :fold].astype(BF16)
    weight = pairs[:, fold : fold + 1] + pairs[:, fold + 1 : fold + 2]
    step = min(512, half)
    for c in range(0, half, step):
        part = jnp.dot(left, wo[:fold, c : c + step], preferred_element_type=F32) + jnp.dot(
            right, wo[fold:, c : c + step], preferred_element_type=F32
        )
        acc[:, :, :, c : c + step] = part.reshape(2, 2, rows // 4, step)

    def swap(slot, send, recv, mask):
        copy = remote(send, recv, rs_ss.at[slot], rs_rs.at[slot], {"dev": flip(me, mask)})
        copy.start()
        return copy

    def reduce_rows():
        s1a[...] = acc[1, :, :, :quarter].astype(BF16)
        one_a = swap(0, s1a, r1a, 1)
        s1b[...] = acc[:, 1, :, quarter:].astype(BF16)
        one_b = swap(1, s1b, r1b, 2)
        one_a.wait()
        s2a[...] = (acc[0, 1, :, :quarter] + r1a[1].astype(F32)).astype(BF16)
        two_a = swap(2, s2a, r2a, 2)
        one_b.wait()
        s2b[...] = (acc[1, 0, :, quarter:] + r1b[1].astype(F32)).astype(BF16)
        two_b = swap(3, s2b, r2b, 1)
        keep_a = acc[0, 0, :, :quarter] + r1a[0].astype(F32)
        keep_b = acc[0, 0, :, quarter:] + r1b[0].astype(F32)
        two_a.wait()
        two_b.wait()
        keep = jnp.concatenate(
            [keep_a + r2a[...].astype(F32), keep_b + r2b[...].astype(F32)], axis=1
        )
        for t in range(tails):
            count = keep.shape[0] // 2
            tail_send[t][...] = keep[count:].astype(BF16)
            copy = swap(4 + t, tail_send[t], tail_recv[t], 4 << t)
            copy.wait()
            keep = keep[:count] + tail_recv[t][...].astype(F32)
        return keep

    attn = reduce_rows()
    swap_res.wait()
    res_other = res_recv[...]
    hidden = attn + jnp.concatenate(
        [jnp.where(first, res_own, res_other), jnp.where(first, res_other, res_own)], axis=0
    )
    square = jnp.sum(hidden * hidden, axis=1, keepdims=True)
    sq_send[...] = jnp.broadcast_to(square, sq_send.shape)
    swap_sq = remote(sq_send, sq_recv, pool_ss.at[2], pool_rs.at[2], mate)
    swap_sq.start()
    gains = gain[...].astype(F32)
    gains = jnp.where(first, gains[:, :half], gains[:, half:])
    swap_sq.wait()
    mean_square = (square + sq_recv[:, :1]) / (2 * half)
    normed = (hidden * lax.rsqrt(mean_square + 1e-06) * gains).astype(BF16)
    gathered[0, 0, :ROW] = normed

    def gather(slot, view, target, mask):
        copy = remote(view, target, ag_ss.at[slot], ag_rs.at[slot], {"dev": flip(me, mask)})
        copy.start()
        return copy

    passed = []

    def pass_on(slot, index):
        copy = remote(
            gathered.at[index], other.at[index], pool_ss.at[slot], pool_rs.at[slot], mate
        )
        copy.start()
        passed.append(copy)

    count = ROW
    for t in range(tails):
        copy = gather(
            t,
            gathered.at[0, 0, pl.ds(0, count)],
            gathered.at[0, 0, pl.ds(count, count)],
            4 << (tails - 1 - t),
        )
        copy.wait()
        count *= 2
    side_a, side_b = pl.ds(0, quarter), pl.ds(quarter, quarter)
    whole = slice(None)
    one_a = gather(tails, gathered.at[0, 0, :, side_a], gathered.at[0, 1, :, side_a], 2)
    one_b = gather(tails + 1, gathered.at[0, 0, :, side_b], gathered.at[1, 0, :, side_b], 1)
    pass_on(3, (0, 0))
    one_a.wait()
    two_a = gather(tails + 2, gathered.at[0, :, :, side_a], gathered.at[1, :, :, side_a], 1)
    one_b.wait()
    two_b = gather(tails + 3, gathered.at[:, 0, :, side_b], gathered.at[:, 1, :, side_b], 2)
    pass_on(4, (0, 1, whole, side_a))
    pass_on(5, (1, 0, whole, side_b))
    two_a.wait()
    pass_on(6, (1, whole, whole, side_a))
    two_b.wait()
    pass_on(7, (whole, 1, whole, side_b))

    for load in loads[1:7]:
        load.wait()
    own_rows = gathered[...].reshape(rows, half)
    gate_proj = jnp.dot(own_rows, wg[0], preferred_element_type=F32)
    up_proj = jnp.dot(own_rows, wu[0], preferred_element_type=F32)
    for copy in passed:
        copy.wait()
    other_rows = other[...].reshape(rows, half)
    gate_proj = gate_proj + jnp.dot(other_rows, wg[1], preferred_element_type=F32)
    up_proj = up_proj + jnp.dot(other_rows, wu[1], preferred_element_type=F32)
    activated = gate_proj / (1.0 + jnp.exp(-gate_proj)) * up_proj
    activated = (activated * weight).astype(BF16)
    for c in range(0, half, step):
        part = jnp.dot(activated, wd[1, :, c : c + step], preferred_element_type=F32)
        pool_send[:, :, :, c : c + step] = part.astype(BF16).reshape(2, 2, rows // 4, step)
    swap_pool = remote(pool_send, pool_recv, pool_ss.at[8], pool_rs.at[8], mate)
    swap_pool.start()
    for c in range(0, half, step):
        part = jnp.dot(activated, wd[0, :, c : c + step], preferred_element_type=F32)
        acc[:, :, :, c : c + step] = part.reshape(2, 2, rows // 4, step)
    swap_pool.wait()
    acc[...] = acc[...] + pool_recv[...].astype(F32)
    total = hidden + reduce_rows()
    out_send[...] = jnp.where(first, total[8:], total[:8])
    swap_out = remote(out_send, out_recv, pool_ss.at[9], pool_rs.at[9], mate)
    swap_out.start()
    kept = jnp.where(first, total[:8], total[8:])
    swap_out.wait()
    come = out_recv[...]
    out[:, :half] = jnp.where(first, kept, come).astype(BF16)
    out[:, half:] = jnp.where(first, come, kept).astype(BF16)


def local(
    residual_in,
    queries,
    key_cache,
    value_cache,
    new_keys,
    new_values,
    lengths,
    out_weight,
    norm_gain,
    expert_ids,
    route_weights,
    w_gate,
    w_up,
    w_down,
):
    rows, model = residual_in.shape
    n = lax.axis_size("dev")
    bits = n.bit_length() - 1
    width = out_weight.shape[0]
    fold = width // 2
    lanes = (fold + 2 + 127) // 128 * 128
    hidden_units = w_gate.shape[2]
    half = model // 2
    heads_out = attend(queries, key_cache, value_cache, new_keys, new_values, lengths)
    blocks = heads_out.reshape(rows, n, 2, fold).transpose(1, 2, 0, 3).reshape(n, 2 * rows, fold)
    named = expert_ids[:, :, None] == jnp.arange(n, dtype=jnp.int32)[None, None, :]
    dense = jnp.sum(jnp.where(named, route_weights[:, :, None], 0.0), axis=1)
    high = lax.reduce_precision(dense, 8, 7)
    weights = jnp.stack([high, dense - high], axis=-1).astype(BF16).transpose(1, 0, 2)
    weights = jnp.pad(weights, ((0, 0), (0, rows), (0, lanes - fold - 2)))
    heads = jnp.concatenate([blocks, weights], axis=2)

    group = n * ROW // 4
    quarter = half // 2
    first_step = pltpu.VMEM((2, group, quarter), BF16)
    second_step = pltpu.VMEM((group, quarter), BF16)
    tails = [pltpu.VMEM((group >> (t + 1), half), BF16) for t in range(bits - 2)]
    vmem = pl.BlockSpec(memory_space=pltpu.VMEM)
    hbm = pl.BlockSpec(memory_space=pl.ANY)
    dma = pltpu.SemaphoreType.DMA
    return pl.pallas_call(
        functools.partial(layer_kernel, n),
        out_shape=jax.ShapeDtypeStruct((rows, model), BF16),
        in_specs=[hbm, vmem, vmem, hbm, hbm, hbm, hbm],
        out_specs=vmem,
        scratch_shapes=[
            pltpu.VMEM((2, n, ROW, lanes), BF16),
            pltpu.VMEM((width, half), BF16),
            pltpu.VMEM((2, half, hidden_units), BF16),
            pltpu.VMEM((2, half, hidden_units), BF16),
            pltpu.VMEM((2, hidden_units, half), BF16),
            pltpu.VMEM((2, 2, group, half), F32),
            pltpu.VMEM((2, 2, group, half), BF16),
            pltpu.VMEM((2, 2, group, half), BF16),
            pltpu.VMEM((2, 2, group, half), BF16),
            pltpu.VMEM((2, 2, group, half), BF16),
            pltpu.VMEM((rows, half), F32),
            pltpu.VMEM((rows, half), F32),
            pltpu.VMEM((ROW, 128), F32),
            pltpu.VMEM((ROW, 128), F32),
            pltpu.VMEM((rows, half), F32),
            pltpu.VMEM((rows, half), F32),
            first_step,
            first_step,
            first_step,
            first_step,
            second_step,
            second_step,
            second_step,
            second_step,
            *tails,
            *tails,
            dma((8,)),
            dma((n,)),
            dma((n,)),
            dma((10,)),
            dma((10,)),
            dma((bits + 2,)),
            dma((bits + 2,)),
            dma((bits + 2,)),
            dma((bits + 2,)),
        ],
        compiler_params=pltpu.CompilerParams(
            collective_id=0, has_side_effects=True, vmem_limit_bytes=60 * 1024 * 1024
        ),
    )(heads, residual_in, norm_gain.reshape(1, model), out_weight, w_gate, w_up, w_down)


def solution(mesh):
    placed = (
        P(("groups", "pool", "dev"), None),
        P(("groups", "pool", "dev"), None),
        P(("groups", "pool", "dev"), None, None),
        P(("groups", "pool", "dev"), None, None),
        P(("groups", "pool", "dev"), None),
        P(("groups", "pool", "dev"), None),
        P(("groups", "pool", "dev")),
        P("dev", None),
        P(),
        P(("groups", "pool", "dev"), None),
        P(("groups", "pool", "dev"), None),
        P("dev", None, "pool"),
        P("dev", None, "pool"),
        P("dev", "pool", None),
    )
    return jax.shard_map(
        local,
        mesh=mesh,
        in_specs=placed,
        out_specs=P(("groups", "pool", "dev"), None),
        check_vma=False,
    )
```

time: 193 us -> 96.9 us (0.50)
  waiting for transfers between devices: 110 us -> 0 us
  Pallas kernels: 0 us -> 86.6 us
  blocking collectives: 30.9 us -> 0 us
  matrix products: 21.7 us -> 4.4 us
  between operations: 13.2 us -> 0.1 us
  starting transfers between devices: 6.89 us -> 0 us
  local copies, waits for them, and re-layouts: 6.51 us -> 2.85 us
    reduce_scatter x2 -> x0, waiting for transfers between devices: 86.7 us -> none  [the longest x1 76.9 us: local(): lax.psum_scatter(jnp.dot(regrouped, out_weight, preferred_element_type=jn...]
    pallas_call x0 -> x1, Pallas kernels: none -> 86.6 us  [local(): pl.pallas_call(functools.partial(layer_kernel, n), out_shape=jax.ShapeDty...]
    all_to_all x2 -> x0, blocking collectives: 30.9 us -> none  [the longest x1 15.9 us: local(): lax.all_to_all(heads_out, 'dev', split_axis=1, concat_axis=0, tiled=True)]
    dot_general x7 -> x0, matrix products: 16.8 us -> none  [the longest x1 4.63 us: local(): jnp.dot(activated, w_down[0], preferred_element_type=jnp.float32)]
    all_to_all x1 -> x0, waiting for transfers between devices: 15.3 us -> none  [local(): lax.all_to_all(summed, 'dev', split_axis=0, concat_axis=0, tiled=True)]
    all_gather x1 -> x0, waiting for transfers between devices: 7.53 us -> none  [local(): block = lax.all_gather(arrived, 'pool', axis=0, tiled=True)]
    all_to_all x1 -> x0, starting transfers between devices: 6.81 us -> none  [local(): lax.all_to_all(summed, 'dev', split_axis=0, concat_axis=0, tiled=True)]
    all_to_all x3 -> x0, local copies, waits for them, and re-layouts: 6.05 us -> none  [the longest x2 4 us: local(): lax.all_to_all(outgoing, 'dev', split_axis=0, concat_axis=0, tiled=True)]
  transfers between devices with their start and end apart: 4 -> 0, of which waited for: 4 -> 0; matrix products, arithmetic and copies ran while one was open for 1% -> 0% of each run, Pallas kernels for 0% -> 0%
where the time goes in v1:
time: 96.9 us; the launch traced here: 96.5 us
  Pallas kernels  86.6 us (89%)
  matrix products  4.4 us (5%)
  local copies, waits for them, and re-layouts  2.85 us (3%)
  other arithmetic  2.63 us (3%)
    pallas_call x1, Pallas kernels, local(): pl.pallas_call(functools.partial(layer_kernel, n), out_shape=jax.ShapeDty...  86.6 us

profile of v1, /device:TPU:0, one launch (start us, length us, event | category | flops | bytes accessed | tf_op | source)
XLA Modules:
  0.0 96.5 jit_solution(8297528663546965499)
XLA Ops:
  0.0 0.0 copy-start
  0.0 0.0 copy-start.3
  0.0 0.0 copy-start.2
  0.0 0.0 copy-start.1
  0.0 0.8 iota_compare_fusion.2
  0.8 0.4 copy-done
  1.2 1.6 %fusion.21 = (f32[8,4,16]{2,1,0:T(4,128)S(1)}, f32[8,4,16,128]{3,2,1,0:T(8,128)S(1)}) fusion(bf16[8,4,16,128]{3,0,2,1:T(8,128)(2,1)} %bitcast.37, pred[8,128]{1,0:T(8,128)(4,1)S(1)} %iota_compare_fusion.2, bf16[8,128,512]{2,1,0:T(8,128)(2,1)S(1)} %copy-done), kind=kOutput, calls=%fused_computation.37 | convolution fusion | flops 16973312 | bytes 1444864 | tf_op jit(solution)/shard_map/rkgd,rlkd->rkgl/dot_general | solution.py:26
  2.9 1.1 %fusion.13 = f32[8,4,1,16]{3,2,1,0:T(1,128)S(1)} fusion(bf16[8,4,16,128]{3,0,2,1:T(8,128)(2,1)} %bitcast.38, bf16[8,4,128,1]{2,0,1,3:T(8,128)(2,1)} %bitcast.42), kind=kOutput, calls=%fused_computation.19 | convolution fusion | flops 131072 | bytes 141312 | tf_op jit(solution)/shard_map/rkgd,rkd->rkg/dot_general | solution.py:30
  4.0 0.3 fusion.7
  4.3 0.7 bitcast_convert_fusion
  5.0 1.7 %fusion.1 = bf16[8,4,16,128]{3,2,1,0:T(8,128)(2,1)S(1)} fusion(f32[8,4,16,128]{3,2,1,0:T(8,128)S(1)} %get-tuple-element.10, f32[8,4,128]{2,1,0:T(4,128)S(1)} %copy.31, f32[8,4,16]{2,1,0:T(4,128)S(1)} %get-tuple-element.6, f32[8,4,16]{2,1,0:T(4,128)S(1)} %get-tuple-element.5, f32[8,4,16]{2,1,0:T(4,128)S(1)} %multiply_maximum_fusion, ...), kind=kOutput, calls=%fused_computation.3 | convolution fusion | flops 17235968 | bytes 1465344 | tf_op jit(solution)/shard_map/rkgl,rlkd->rkgd/dot_general | solution.py:46
  6.7 0.1 convert_element_type.36
  6.8 0.1 copy.57
  6.9 0.0 copy-done.3
  6.9 0.0 copy-done.2
  6.9 0.1 select_reduce_fusion
  7.0 0.1 copy.33
  7.2 0.7 fusion.8.refs_0_
  7.9 0.0 copy-done.1
  7.9 0.6 reshape.73.refs_2_
  8.5 86.6 %shard_map.136 = bf16[8,4096]{1,0:T(8,128)(2,1)} custom-call(bf16[16,16,384]{2,1,0:T(8,128)(2,1)} %fusion.8.refs_0_, bf16[8,4096]{1,0:T(8,128)(2,1)} %refs_1_.1, bf16[1,4096]{1,0:T(2,128)(2,1)} %reshape.73.refs_2_, bf16[512,4096]{1,0:T(8,128)(2,1)} %refs_3_.1, bf16[1,4096,384]{2,1,0:T(8,128)(2,1)} %refs_4_.1, bf16[1,4096,384]{2,1,0:T(8,128)(2,1)} %refs_5_.1, ...), custom_call_target="tpu_custom_call" | custom-call | tf_op jit(solution)/shard_map/pallas_call | solution.py:340
  95.1 1.5 %copy.59 = bf16[8,4096]{1,0:T(8,128)(2,1)} copy(bf16[8,4096]{1,0:T(8,128)(2,1)} %shard_map.136) | data formatting | bytes 131072
  (5 shorter events, 0.1 us)
Async XLA Ops:
  0.0 1.2 %copy-start = (bf16[8,128,512]{2,1,0:T(8,128)(2,1)S(1)}, bf16[8,128,512]{2,1,0:T(8,128)(2,1)}, u32[]{:S(2)}) copy-start(bf16[8,128,512]{2,1,0:T(8,128)(2,1)} %param.16) | copy-start | bytes 3145732
  0.0 6.9 %copy-start.3 = (s32[8,8]{1,0:T(8,128)S(1)}, s32[8,8]{1,0:T(8,128)}, u32[]{:S(2)}) copy-start(s32[8,8]{1,0:T(8,128)} %param.23) | copy-start | bytes 772
  0.0 6.9 %copy-start.2 = (f32[8,8]{1,0:T(8,128)S(1)}, f32[8,8]{1,0:T(8,128)}, u32[]{:S(2)}) copy-start(f32[8,8]{1,0:T(8,128)} %param.24) | copy-start | bytes 772
  0.0 7.9 %copy-start.1 = (bf16[4096]{0:T(1024)(128)(2,1)S(1)}, bf16[4096]{0:T(1024)(128)(2,1)}, u32[]{:S(2)}) copy-start(bf16[4096]{0:T(1024)(128)(2,1)} %param.22) | copy-start | bytes 24580

commit v2 on v1

--- a/solution.py
+++ b/solution.py
@@ -53,6 +53,7 @@
 F32 = jnp.float32
 BF16 = jnp.bfloat16
 ROW = 16
+PIECES = 2
 
 
 def flip(index, mask):
@@ -77,11 +78,12 @@
         return taken
 
     heads, residual, gain, wo_hbm, wg_hbm, wu_hbm, wd_hbm, out = take(8)
-    hb, wo, wg, wu, wd, acc, gathered, other, pool_send, pool_recv = take(10)
+    hb, wo, wg, wu, wd, acc, gathered, other, pool_recv = take(9)
     res_send, res_recv, sq_send, sq_recv, out_send, out_recv = take(6)
-    s1a, s1b, r1a, r1b, s2a, s2b, r2a, r2b = take(8)
+    s1, r1, s2, r2 = take(4)
     tail_send, tail_recv = take(tails), take(tails)
     local_sem, heads_ss, heads_rs, pool_ss, pool_rs, rs_ss, rs_rs, ag_ss, ag_rs = take(9)
+    pass_ss, pass_rs, mix_ss, mix_rs = take(4)
 
     me = lax.axis_index("dev")
     pool = lax.axis_index("pool")
@@ -168,45 +170,58 @@
     left = pairs[:, :fold].astype(BF16)
     right = lower[:, :fold].astype(BF16)
     weight = pairs[:, fold : fold + 1] + pairs[:, fold + 1 : fold + 2]
-    step = min(512, half)
-    for c in range(0, half, step):
-        part = jnp.dot(left, wo[:fold, c : c + step], preferred_element_type=F32) + jnp.dot(
-            right, wo[fold:, c : c + step], preferred_element_type=F32
-        )
-        acc[:, :, :, c : c + step] = part.reshape(2, 2, rows // 4, step)
-
-    def swap(slot, send, recv, mask):
-        copy = remote(send, recv, rs_ss.at[slot], rs_rs.at[slot], {"dev": flip(me, mask)})
-        copy.start()
-        return copy
-
-    def reduce_rows():
-        s1a[...] = acc[1, :, :, :quarter].astype(BF16)
-        one_a = swap(0, s1a, r1a, 1)
-        s1b[...] = acc[:, 1, :, quarter:].astype(BF16)
-        one_b = swap(1, s1b, r1b, 2)
-        one_a.wait()
-        s2a[...] = (acc[0, 1, :, :quarter] + r1a[1].astype(F32)).astype(BF16)
-        two_a = swap(2, s2a, r2a, 2)
-        one_b.wait()
-        s2b[...] = (acc[1, 0, :, quarter:] + r1b[1].astype(F32)).astype(BF16)
-        two_b = swap(3, s2b, r2b, 1)
-        keep_a = acc[0, 0, :, :quarter] + r1a[0].astype(F32)
-        keep_b = acc[0, 0, :, quarter:] + r1b[0].astype(F32)
-        two_a.wait()
-        two_b.wait()
-        keep = jnp.concatenate(
-            [keep_a + r2a[...].astype(F32), keep_b + r2b[...].astype(F32)], axis=1
-        )
-        for t in range(tails):
-            count = keep.shape[0] // 2
-            tail_send[t][...] = keep[count:].astype(BF16)
-            copy = swap(4 + t, tail_send[t], tail_recv[t], 4 << t)
-            copy.wait()
-            keep = keep[:count] + tail_recv[t][...].astype(F32)
-        return keep
-
-    attn = reduce_rows()
+    chunk = quarter // PIECES
+    pieces = []
+    for k in range(PIECES):
+        pieces.append((0, pl.ds(k * chunk, chunk)))
+        pieces.append((1, pl.ds(quarter + k * chunk, chunk)))
+    near = [(1, 2), (2, 1)]
+
+    def project(c, cols):
+        part = jnp.dot(left, wo[:fold, cols], preferred_element_type=F32) + jnp.dot(
+            right, wo[fold:, cols], preferred_element_type=F32
+        )
+        acc[:, :, :, cols] = part.reshape(2, 2, rows // 4, chunk)
+
+    def reduce_rows(prepare):
+        def swap(c, stage, send, recv, mask):
+            copy = remote(
+                send, recv, rs_ss.at[c, stage], rs_rs.at[c, stage], {"dev": flip(me, mask)}
+            )
+            copy.start()
+            return copy
+
+        flying = []
+        for c, (side, cols) in enumerate(pieces):
+            prepare(c, cols)
+            gone = acc[:, 1, :, cols] if side else acc[1, :, :, cols]
+            s1[c] = gone.astype(BF16)
+            flying.append(swap(c, 0, s1.at[c], r1.at[c], near[side][0]))
+        for c, (side, cols) in enumerate(pieces):
+            flying[c].wait()
+            gone = acc[1, 0, :, cols] if side else acc[0, 1, :, cols]
+            s2[c] = (gone + r1[c, 1].astype(F32)).astype(BF16)
+            flying[c] = swap(c, 1, s2.at[c], r2.at[c], near[side][1])
+            acc[0, 0, :, cols] = acc[0, 0, :, cols] + r1[c, 0].astype(F32)
+        keeps = []
+        for t in range(tails + 1):
+            for c, (side, cols) in enumerate(pieces):
+                flying[c].wait()
+                if t == 0:
+                    keep = acc[0, 0, :, cols] + r2[c].astype(F32)
+                else:
+                    count = (rows // 4) >> t
+                    keep = acc[0, 0, :count, cols] + tail_recv[t - 1][c].astype(F32)
+                if t == tails:
+                    keeps.append(keep)
+                    continue
+                count = (rows // 4) >> (t + 1)
+                tail_send[t][c] = keep[count:].astype(BF16)
+                flying[c] = swap(c, 2 + t, tail_send[t].at[c], tail_recv[t].at[c], 4 << t)
+                acc[0, 0, :count, cols] = keep[:count]
+        return jnp.concatenate(keeps[0::2] + keeps[1::2], axis=1)
+
+    attn = reduce_rows(project)
     swap_res.wait()
     res_other = res_recv[...]
     hidden = attn + jnp.concatenate(
@@ -223,71 +238,89 @@
     normed = (hidden * lax.rsqrt(mean_square + 1e-06) * gains).astype(BF16)
     gathered[0, 0, :ROW] = normed
 
-    def gather(slot, view, target, mask):
-        copy = remote(view, target, ag_ss.at[slot], ag_rs.at[slot], {"dev": flip(me, mask)})
+    def gather(c, stage, view, target, mask):
+        copy = remote(view, target, ag_ss.at[c, stage], ag_rs.at[c, stage], {"dev": flip(me, mask)})
         copy.start()
         return copy
 
-    passed = []
-
-    def pass_on(slot, index):
+    passed = [[] for _ in pieces]
+
+    def pass_on(c, slot, index):
         copy = remote(
-            gathered.at[index], other.at[index], pool_ss.at[slot], pool_rs.at[slot], mate
+            gathered.at[index], other.at[index], pass_ss.at[c, slot], pass_rs.at[c, slot], mate
         )
         copy.start()
-        passed.append(copy)
-
-    count = ROW
+        passed[c].append(copy)
+
+    whole = slice(None)
+    flying = [None] * len(pieces)
     for t in range(tails):
-        copy = gather(
-            t,
-            gathered.at[0, 0, pl.ds(0, count)],
-            gathered.at[0, 0, pl.ds(count, count)],
-            4 << (tails - 1 - t),
-        )
-        copy.wait()
-        count *= 2
-    side_a, side_b = pl.ds(0, quarter), pl.ds(quarter, quarter)
-    whole = slice(None)
-    one_a = gather(tails, gathered.at[0, 0, :, side_a], gathered.at[0, 1, :, side_a], 2)
-    one_b = gather(tails + 1, gathered.at[0, 0, :, side_b], gathered.at[1, 0, :, side_b], 1)
-    pass_on(3, (0, 0))
-    one_a.wait()
-    two_a = gather(tails + 2, gathered.at[0, :, :, side_a], gathered.at[1, :, :, side_a], 1)
-    one_b.wait()
-    two_b = gather(tails + 3, gathered.at[:, 0, :, side_b], gathered.at[:, 1, :, side_b], 2)
-    pass_on(4, (0, 1, whole, side_a))
-    pass_on(5, (1, 0, whole, side_b))
-    two_a.wait()
-    pass_on(6, (1, whole, whole, side_a))
-    two_b.wait()
-    pass_on(7, (whole, 1, whole, side_b))
-
+        count = ROW << t
+        for c, (side, cols) in enumerate(pieces):
+            if t:
+                flying[c].wait()
+            flying[c] = gather(
+                c,
+                t,
+                gathered.at[0, 0, pl.ds(0, count), cols],
+                gathered.at[0, 0, pl.ds(count, count), cols],
+                4 << (tails - 1 - t),
+            )
+    for c, (side, cols) in enumerate(pieces):
+        flying[c].wait()
+        flying[c] = gather(
+            c,
+            tails,
+            gathered.at[0, 0, :, cols],
+            gathered.at[1, 0, :, cols] if side else gathered.at[0, 1, :, cols],
+            near[side][1],
+        )
+        pass_on(c, 0, (0, 0, whole, cols))
+    for c, (side, cols) in enumerate(pieces):
+        flying[c].wait()
+        flying[c] = gather(
+            c,
+            tails + 1,
+            gathered.at[:, 0, :, cols] if side else gathered.at[0, :, :, cols],
+            gathered.at[:, 1, :, cols] if side else gathered.at[1, :, :, cols],
+            near[side][0],
+        )
+        pass_on(c, 1, (1, 0, whole, cols) if side else (0, 1, whole, cols))
     for load in loads[1:7]:
         load.wait()
-    own_rows = gathered[...].reshape(rows, half)
-    gate_proj = jnp.dot(own_rows, wg[0], preferred_element_type=F32)
-    up_proj = jnp.dot(own_rows, wu[0], preferred_element_type=F32)
-    for copy in passed:
-        copy.wait()
-    other_rows = other[...].reshape(rows, half)
-    gate_proj = gate_proj + jnp.dot(other_rows, wg[1], preferred_element_type=F32)
-    up_proj = up_proj + jnp.dot(other_rows, wu[1], preferred_element_type=F32)
+    gate_proj = jnp.zeros((rows, wg.shape[-1]), F32)
+    up_proj = gate_proj
+    for c, (side, cols) in enumerate(pieces):
+        flying[c].wait()
+        pass_on(c, 2, (whole, 1, whole, cols) if side else (1, whole, whole, cols))
+        block = gathered[:, :, :, cols].reshape(rows, chunk)
+        gate_proj = gate_proj + jnp.dot(block, wg[0, cols], preferred_element_type=F32)
+        up_proj = up_proj + jnp.dot(block, wu[0, cols], preferred_element_type=F32)
+    for c, (side, cols) in enumerate(pieces):
+        for copy in passed[c]:
+            copy.wait()
+        block = other[:, :, :, cols].reshape(rows, chunk)
+        gate_proj = gate_proj + jnp.dot(block, wg[1, cols], preferred_element_type=F32)
+        up_proj = up_proj + jnp.dot(block, wu[1, cols], preferred_element_type=F32)
     activated = gate_proj / (1.0 + jnp.exp(-gate_proj)) * up_proj
     activated = (activated * weight).astype(BF16)
-    for c in range(0, half, step):
-        part = jnp.dot(activated, wd[1, :, c : c + step], preferred_element_type=F32)
-        pool_send[:, :, :, c : c + step] = part.astype(BF16).reshape(2, 2, rows // 4, step)
-    swap_pool = remote(pool_send, pool_recv, pool_ss.at[8], pool_rs.at[8], mate)
-    swap_pool.start()
-    for c in range(0, half, step):
-        part = jnp.dot(activated, wd[0, :, c : c + step], preferred_element_type=F32)
-        acc[:, :, :, c : c + step] = part.reshape(2, 2, rows // 4, step)
-    swap_pool.wait()
-    acc[...] = acc[...] + pool_recv[...].astype(F32)
-    total = hidden + reduce_rows()
+    mixes = []
+    for c, (side, cols) in enumerate(pieces):
+        part = jnp.dot(activated, wd[1, :, cols], preferred_element_type=F32)
+        sent = gathered.at[:, :, :, cols]
+        sent[...] = part.astype(BF16).reshape(2, 2, rows // 4, chunk)
+        mixes.append(remote(sent, pool_recv.at[c], mix_ss.at[c], mix_rs.at[c], mate))
+        mixes[-1].start()
+
+    def mix(c, cols):
+        part = jnp.dot(activated, wd[0, :, cols], preferred_element_type=F32)
+        mixes[c].wait()
+        part = part.reshape(2, 2, rows // 4, chunk)
+        acc[:, :, :, cols] = part + pool_recv[c].astype(F32)
+
+    total = hidden + reduce_rows(mix)
     out_send[...] = jnp.where(first, total[8:], total[:8])
-    swap_out = remote(out_send, out_recv, pool_ss.at[9], pool_rs.at[9], mate)
+    swap_out = remote(out_send, out_recv, pool_ss.at[3], pool_rs.at[3], mate)
     swap_out.start()
     kept = jnp.where(first, total[:8], total[8:])
     swap_out.wait()
@@ -330,10 +363,11 @@
     heads = jnp.concatenate([blocks, weights], axis=2)
 
     group = n * ROW // 4
-    quarter = half // 2
-    first_step = pltpu.VMEM((2, group, quarter), BF16)
-    second_step = pltpu.VMEM((group, quarter), BF16)
-    tails = [pltpu.VMEM((group >> (t + 1), half), BF16) for t in range(bits - 2)]
+    count = 2 * PIECES
+    chunk = half // count
+    first_step = pltpu.VMEM((count, 2, group, chunk), BF16)
+    second_step = pltpu.VMEM((count, group, chunk), BF16)
+    tails = [pltpu.VMEM((count, group >> (t + 1), chunk), BF16) for t in range(bits - 2)]
     vmem = pl.BlockSpec(memory_space=pltpu.VMEM)
     hbm = pl.BlockSpec(memory_space=pl.ANY)
     dma = pltpu.SemaphoreType.DMA
@@ -351,8 +385,7 @@
             pltpu.VMEM((2, 2, group, half), F32),
             pltpu.VMEM((2, 2, group, half), BF16),
             pltpu.VMEM((2, 2, group, half), BF16),
-            pltpu.VMEM((2, 2, group, half), BF16),
-            pltpu.VMEM((2, 2, group, half), BF16),
+            pltpu.VMEM((count, 2, 2, group, chunk), BF16),
             pltpu.VMEM((rows, half), F32),
             pltpu.VMEM((rows, half), F32),
             pltpu.VMEM((ROW, 128), F32),
@@ -361,10 +394,6 @@
             pltpu.VMEM((rows, half), F32),
             first_step,
             first_step,
-            first_step,
-            first_step,
-            second_step,
-            second_step,
             second_step,
             second_step,
             *tails,
@@ -372,12 +401,16 @@
             dma((8,)),
             dma((n,)),
             dma((n,)),
-            dma((10,)),
-            dma((10,)),
-            dma((bits + 2,)),
-            dma((bits + 2,)),
-            dma((bits + 2,)),
-            dma((bits + 2,)),
+            dma((4,)),
+            dma((4,)),
+            dma((count, bits)),
+            dma((count, bits)),
+            dma((count, bits)),
+            dma((count, bits)),
+            dma((count, 3)),
+            dma((count, 3)),
+            dma((count,)),
+            dma((count,)),
         ],
         compiler_params=pltpu.CompilerParams(
             collective_id=0, has_side_effects=True, vmem_limit_bytes=60 * 1024 * 1024

time: 96.9 us -> 87.3 us (0.901)
  Pallas kernels: 86.6 us -> 77 us
    pallas_call x1, Pallas kernels: 86.6 us -> 77 us  [local(): pl.pallas_call(functools.partial(layer_kernel, n), out_shape=jax.ShapeDty...]
where the time goes in v2:
time: 87.3 us; the launch traced here: 87 us
  Pallas kernels  77 us (88%)
  matrix products  4.4 us (5%)
  local copies, waits for them, and re-layouts  2.85 us (3%)
  other arithmetic  2.63 us (3%)
    pallas_call x1, Pallas kernels, local(): pl.pallas_call(functools.partial(layer_kernel, n), out_shape=jax.ShapeDty...  77 us
    unnamed x9, local copies, waits for them, and re-layouts  1.9 us

profile of v2, /device:TPU:0, one launch (start us, length us, event | category | flops | bytes accessed | tf_op | source)
XLA Modules:
  0.0 87.0 jit_solution(5279966972928887414)
XLA Ops:
  0.0 0.0 copy-start
  0.0 0.0 copy-start.3
  0.0 0.0 copy-start.2
  0.0 0.0 copy-start.1
  0.0 0.8 iota_compare_fusion.2
  0.8 0.4 copy-done
  1.2 1.6 %fusion.21 = (f32[8,4,16]{2,1,0:T(4,128)S(1)}, f32[8,4,16,128]{3,2,1,0:T(8,128)S(1)}) fusion(bf16[8,4,16,128]{3,0,2,1:T(8,128)(2,1)} %bitcast.37, pred[8,128]{1,0:T(8,128)(4,1)S(1)} %iota_compare_fusion.2, bf16[8,128,512]{2,1,0:T(8,128)(2,1)S(1)} %copy-done), kind=kOutput, calls=%fused_computation.37 | convolution fusion | flops 16973312 | bytes 1444864 | tf_op jit(solution)/shard_map/rkgd,rlkd->rkgl/dot_general | solution.py:26
  2.9 1.1 %fusion.13 = f32[8,4,1,16]{3,2,1,0:T(1,128)S(1)} fusion(bf16[8,4,16,128]{3,0,2,1:T(8,128)(2,1)} %bitcast.38, bf16[8,4,128,1]{2,0,1,3:T(8,128)(2,1)} %bitcast.42), kind=kOutput, calls=%fused_computation.19 | convolution fusion | flops 131072 | bytes 141312 | tf_op jit(solution)/shard_map/rkgd,rkd->rkg/dot_general | solution.py:30
  4.0 0.3 fusion.7
  4.3 0.7 bitcast_convert_fusion
  5.0 1.7 %fusion.1 = bf16[8,4,16,128]{3,2,1,0:T(8,128)(2,1)S(1)} fusion(f32[8,4,16,128]{3,2,1,0:T(8,128)S(1)} %get-tuple-element.10, f32[8,4,128]{2,1,0:T(4,128)S(1)} %copy.31, f32[8,4,16]{2,1,0:T(4,128)S(1)} %get-tuple-element.6, f32[8,4,16]{2,1,0:T(4,128)S(1)} %get-tuple-element.5, f32[8,4,16]{2,1,0:T(4,128)S(1)} %multiply_maximum_fusion, ...), kind=kOutput, calls=%fused_computation.3 | convolution fusion | flops 17235968 | bytes 1465344 | tf_op jit(solution)/shard_map/rkgl,rlkd->rkgd/dot_general | solution.py:46
  6.7 0.1 convert_element_type.36
  6.8 0.1 copy.57
  6.9 0.0 copy-done.3
  6.9 0.0 copy-done.2
  6.9 0.1 select_reduce_fusion
  7.0 0.1 copy.33
  7.2 0.7 fusion.8.refs_0_
  7.9 0.0 copy-done.1
  7.9 0.6 reshape.73.refs_2_
  8.5 77.0 %shard_map.136 = bf16[8,4096]{1,0:T(8,128)(2,1)} custom-call(bf16[16,16,384]{2,1,0:T(8,128)(2,1)} %fusion.8.refs_0_, bf16[8,4096]{1,0:T(8,128)(2,1)} %refs_1_.1, bf16[1,4096]{1,0:T(2,128)(2,1)} %reshape.73.refs_2_, bf16[512,4096]{1,0:T(8,128)(2,1)} %refs_3_.1, bf16[1,4096,384]{2,1,0:T(8,128)(2,1)} %refs_4_.1, bf16[1,4096,384]{2,1,0:T(8,128)(2,1)} %refs_5_.1, ...), custom_call_target="tpu_custom_call" | custom-call | tf_op jit(solution)/shard_map/pallas_call | solution.py:374
  85.5 1.5 %copy.59 = bf16[8,4096]{1,0:T(8,128)(2,1)} copy(bf16[8,4096]{1,0:T(8,128)(2,1)} %shard_map.136) | data formatting | bytes 131072
  (5 shorter events, 0.1 us)
Async XLA Ops:
  0.0 1.2 %copy-start = (bf16[8,128,512]{2,1,0:T(8,128)(2,1)S(1)}, bf16[8,128,512]{2,1,0:T(8,128)(2,1)}, u32[]{:S(2)}) copy-start(bf16[8,128,512]{2,1,0:T(8,128)(2,1)} %param.16) | copy-start | bytes 3145732
  0.0 6.9 %copy-start.3 = (s32[8,8]{1,0:T(8,128)S(1)}, s32[8,8]{1,0:T(8,128)}, u32[]{:S(2)}) copy-start(s32[8,8]{1,0:T(8,128)} %param.23) | copy-start | bytes 772
  0.0 6.9 %copy-start.2 = (f32[8,8]{1,0:T(8,128)S(1)}, f32[8,8]{1,0:T(8,128)}, u32[]{:S(2)}) copy-start(f32[8,8]{1,0:T(8,128)} %param.24) | copy-start | bytes 772
  0.0 7.9 %copy-start.1 = (bf16[4096]{0:T(1024)(128)(2,1)S(1)}, bf16[4096]{0:T(1024)(128)(2,1)}, u32[]{:S(2)}) copy-start(bf16[4096]{0:T(1024)(128)(2,1)} %param.22) | copy-start | bytes 24580

commit v3 on v2

--- a/solution.py
+++ b/solution.py
@@ -67,9 +67,14 @@
     return sum(((value >> bit) & 1) << (bits - 1 - bit) for bit in range(bits))
 
 
+def grouped(bits):
+    return [(bit, min(2, bits - bit)) for bit in range(2, bits, 2)]
+
+
 def layer_kernel(n, *refs):
     bits = n.bit_length() - 1
-    tails = bits - 2
+    groups = grouped(bits)
+    tails = len(groups)
     refs = list(refs)
 
     def take(count):
@@ -204,21 +209,30 @@
             flying[c] = swap(c, 1, s2.at[c], r2.at[c], near[side][1])
             acc[0, 0, :, cols] = acc[0, 0, :, cols] + r1[c, 0].astype(F32)
         keeps = []
+        count, slot = rows // 4, 2
         for t in range(tails + 1):
+            bit, size = groups[t] if t < tails else (0, 0)
+            below = count >> size
             for c, (side, cols) in enumerate(pieces):
-                flying[c].wait()
                 if t == 0:
+                    flying[c].wait()
                     keep = acc[0, 0, :, cols] + r2[c].astype(F32)
                 else:
-                    count = (rows // 4) >> t
-                    keep = acc[0, 0, :count, cols] + tail_recv[t - 1][c].astype(F32)
+                    keep = acc[0, 0, :count, cols]
+                    for q, copy in enumerate(flying[c]):
+                        copy.wait()
+                        keep = keep + tail_recv[t - 1][c, q].astype(F32)
                 if t == tails:
                     keeps.append(keep)
                     continue
-                count = (rows // 4) >> (t + 1)
-                tail_send[t][c] = keep[count:].astype(BF16)
-                flying[c] = swap(c, 2 + t, tail_send[t].at[c], tail_recv[t].at[c], 4 << t)
-                acc[0, 0, :count, cols] = keep[:count]
+                flying[c] = []
+                for q in range(1, 1 << size):
+                    send, recv = tail_send[t].at[c, q - 1], tail_recv[t].at[c, q - 1]
+                    send[...] = keep[q * below : (q + 1) * below].astype(BF16)
+                    mask = reverse_bits(q, size) << bit
+                    flying[c].append(swap(c, slot + q - 1, send, recv, mask))
+                acc[0, 0, :below, cols] = keep[:below]
+            count, slot = below, slot + (1 << size) - 1
         return jnp.concatenate(keeps[0::2] + keeps[1::2], axis=1)
 
     attn = reduce_rows(project)
@@ -253,24 +267,29 @@
         passed[c].append(copy)
 
     whole = slice(None)
-    flying = [None] * len(pieces)
-    for t in range(tails):
-        count = ROW << t
+    flying = [[] for _ in pieces]
+    count, slot = ROW, 2
+    for bit, size in groups[::-1]:
         for c, (side, cols) in enumerate(pieces):
-            if t:
-                flying[c].wait()
-            flying[c] = gather(
-                c,
-                t,
-                gathered.at[0, 0, pl.ds(0, count), cols],
-                gathered.at[0, 0, pl.ds(count, count), cols],
-                4 << (tails - 1 - t),
-            )
+            for copy in flying[c]:
+                copy.wait()
+            flying[c] = [
+                gather(
+                    c,
+                    slot + q - 1,
+                    gathered.at[0, 0, pl.ds(0, count), cols],
+                    gathered.at[0, 0, pl.ds(q * count, count), cols],
+                    reverse_bits(q, size) << bit,
+                )
+                for q in range(1, 1 << size)
+            ]
+        count, slot = count << size, slot + (1 << size) - 1
     for c, (side, cols) in enumerate(pieces):
-        flying[c].wait()
+        for copy in flying[c]:
+            copy.wait()
         flying[c] = gather(
             c,
-            tails,
+            0,
             gathered.at[0, 0, :, cols],
             gathered.at[1, 0, :, cols] if side else gathered.at[0, 1, :, cols],
             near[side][1],
@@ -280,7 +299,7 @@
         flying[c].wait()
         flying[c] = gather(
             c,
-            tails + 1,
+            1,
             gathered.at[:, 0, :, cols] if side else gathered.at[0, :, :, cols],
             gathered.at[:, 1, :, cols] if side else gathered.at[1, :, :, cols],
             near[side][0],
@@ -367,7 +386,11 @@
     chunk = half // count
     first_step = pltpu.VMEM((count, 2, group, chunk), BF16)
     second_step = pltpu.VMEM((count, group, chunk), BF16)
-    tails = [pltpu.VMEM((count, group >> (t + 1), chunk), BF16) for t in range(bits - 2)]
+    tails, below, slots = [], group, 2
+    for _, size in grouped(bits):
+        below = below >> size
+        tails.append(pltpu.VMEM((count, (1 << size) - 1, below, chunk), BF16))
+        slots += (1 << size) - 1
     vmem = pl.BlockSpec(memory_space=pltpu.VMEM)
     hbm = pl.BlockSpec(memory_space=pl.ANY)
     dma = pltpu.SemaphoreType.DMA
@@ -403,10 +426,10 @@
             dma((n,)),
             dma((4,)),
             dma((4,)),
-            dma((count, bits)),
-            dma((count, bits)),
-            dma((count, bits)),
-            dma((count, bits)),
+            dma((count, slots)),
+            dma((count, slots)),
+            dma((count, slots)),
+            dma((count, slots)),
             dma((count, 3)),
             dma((count, 3)),
             dma((count,)),

time: 87.3 us -> 83.7 us (0.959)
  Pallas kernels: 77 us -> 73.4 us
    pallas_call x1, Pallas kernels: 77 us -> 73.4 us  [local(): pl.pallas_call(functools.partial(layer_kernel, n), out_shape=jax.ShapeDty...]
where the time goes in v3:
time: 83.7 us; the launch traced here: 83.4 us
  Pallas kernels  73.4 us (88%)
  matrix products  4.4 us (5%)
  local copies, waits for them, and re-layouts  2.85 us (3%)
  other arithmetic  2.63 us (3%)
    pallas_call x1, Pallas kernels, local(): pl.pallas_call(functools.partial(layer_kernel, n), out_shape=jax.ShapeDty...  73.4 us
    unnamed x9, local copies, waits for them, and re-layouts  1.9 us

profile of v3, /device:TPU:0, one launch (start us, length us, event | category | flops | bytes accessed | tf_op | source)
XLA Modules:
  0.0 83.4 jit_solution(174469959679222960)
XLA Ops:
  0.0 0.0 copy-start
  0.0 0.0 copy-start.3
  0.0 0.0 copy-start.2
  0.0 0.0 copy-start.1
  0.0 0.8 iota_compare_fusion.2
  0.8 0.4 copy-done
  1.2 1.6 %fusion.21 = (f32[8,4,16]{2,1,0:T(4,128)S(1)}, f32[8,4,16,128]{3,2,1,0:T(8,128)S(1)}) fusion(bf16[8,4,16,128]{3,0,2,1:T(8,128)(2,1)} %bitcast.37, pred[8,128]{1,0:T(8,128)(4,1)S(1)} %iota_compare_fusion.2, bf16[8,128,512]{2,1,0:T(8,128)(2,1)S(1)} %copy-done), kind=kOutput, calls=%fused_computation.37 | convolution fusion | flops 16973312 | bytes 1444864 | tf_op jit(solution)/shard_map/rkgd,rlkd->rkgl/dot_general | solution.py:26
  2.9 1.1 %fusion.13 = f32[8,4,1,16]{3,2,1,0:T(1,128)S(1)} fusion(bf16[8,4,16,128]{3,0,2,1:T(8,128)(2,1)} %bitcast.38, bf16[8,4,128,1]{2,0,1,3:T(8,128)(2,1)} %bitcast.42), kind=kOutput, calls=%fused_computation.19 | convolution fusion | flops 131072 | bytes 141312 | tf_op jit(solution)/shard_map/rkgd,rkd->rkg/dot_general | solution.py:30
  4.0 0.3 fusion.7
  4.3 0.7 bitcast_convert_fusion
  5.0 1.7 %fusion.1 = bf16[8,4,16,128]{3,2,1,0:T(8,128)(2,1)S(1)} fusion(f32[8,4,16,128]{3,2,1,0:T(8,128)S(1)} %get-tuple-element.10, f32[8,4,128]{2,1,0:T(4,128)S(1)} %copy.31, f32[8,4,16]{2,1,0:T(4,128)S(1)} %get-tuple-element.6, f32[8,4,16]{2,1,0:T(4,128)S(1)} %get-tuple-element.5, f32[8,4,16]{2,1,0:T(4,128)S(1)} %multiply_maximum_fusion, ...), kind=kOutput, calls=%fused_computation.3 | convolution fusion | flops 17235968 | bytes 1465344 | tf_op jit(solution)/shard_map/rkgl,rlkd->rkgd/dot_general | solution.py:46
  6.7 0.1 convert_element_type.36
  6.8 0.1 copy.57
  6.9 0.0 copy-done.3
  6.9 0.0 copy-done.2
  6.9 0.1 select_reduce_fusion
  7.0 0.1 copy.33
  7.2 0.7 fusion.8.refs_0_
  7.9 0.0 copy-done.1
  7.9 0.6 reshape.73.refs_2_
  8.5 73.4 %shard_map.136 = bf16[8,4096]{1,0:T(8,128)(2,1)} custom-call(bf16[16,16,384]{2,1,0:T(8,128)(2,1)} %fusion.8.refs_0_, bf16[8,4096]{1,0:T(8,128)(2,1)} %refs_1_.1, bf16[1,4096]{1,0:T(2,128)(2,1)} %reshape.73.refs_2_, bf16[512,4096]{1,0:T(8,128)(2,1)} %refs_3_.1, bf16[1,4096,384]{2,1,0:T(8,128)(2,1)} %refs_4_.1, bf16[1,4096,384]{2,1,0:T(8,128)(2,1)} %refs_5_.1, ...), custom_call_target="tpu_custom_call" | custom-call | tf_op jit(solution)/shard_map/pallas_call | solution.py:397
  81.9 1.5 %copy.59 = bf16[8,4096]{1,0:T(8,128)(2,1)} copy(bf16[8,4096]{1,0:T(8,128)(2,1)} %shard_map.136) | data formatting | bytes 131072
  (5 shorter events, 0.1 us)
Async XLA Ops:
  0.0 1.2 %copy-start = (bf16[8,128,512]{2,1,0:T(8,128)(2,1)S(1)}, bf16[8,128,512]{2,1,0:T(8,128)(2,1)}, u32[]{:S(2)}) copy-start(bf16[8,128,512]{2,1,0:T(8,128)(2,1)} %param.16) | copy-start | bytes 3145732
  0.0 6.9 %copy-start.3 = (s32[8,8]{1,0:T(8,128)S(1)}, s32[8,8]{1,0:T(8,128)}, u32[]{:S(2)}) copy-start(s32[8,8]{1,0:T(8,128)} %param.23) | copy-start | bytes 772
  0.0 6.9 %copy-start.2 = (f32[8,8]{1,0:T(8,128)S(1)}, f32[8,8]{1,0:T(8,128)}, u32[]{:S(2)}) copy-start(f32[8,8]{1,0:T(8,128)} %param.24) | copy-start | bytes 772
  0.0 7.9 %copy-start.1 = (bf16[4096]{0:T(1024)(128)(2,1)S(1)}, bf16[4096]{0:T(1024)(128)(2,1)}, u32[]{:S(2)}) copy-start(bf16[4096]{0:T(1024)(128)(2,1)} %param.22) | copy-start | bytes 24580

commit v4 on v3

--- a/solution.py
+++ b/solution.py
@@ -164,8 +164,6 @@
         send.wait_recv()
     forward = remote(hb.at[pool], hb.at[pool], pool_ss.at[1], pool_rs.at[1], mate)
     forward.start()
-    for send in sends:
-        send.wait_send()
     loads[0].wait()
     forward.wait()
 
@@ -236,6 +234,8 @@
         return jnp.concatenate(keeps[0::2] + keeps[1::2], axis=1)
 
     attn = reduce_rows(project)
+    for send in sends:
+        send.wait_send()
     swap_res.wait()
     res_other = res_recv[...]
     hidden = attn + jnp.concatenate(
@@ -245,7 +245,7 @@
     sq_send[...] = jnp.broadcast_to(square, sq_send.shape)
     swap_sq = remote(sq_send, sq_recv, pool_ss.at[2], pool_rs.at[2], mate)
     swap_sq.start()
-    gains = gain[...].astype(F32)
+    gains = gain[...].astype(F32).reshape(1, 2 * half)
     gains = jnp.where(first, gains[:, :half], gains[:, half:])
     swap_sq.wait()
     mean_square = (square + sq_recv[:, :1]) / (2 * half)
@@ -438,7 +438,7 @@
         compiler_params=pltpu.CompilerParams(
             collective_id=0, has_side_effects=True, vmem_limit_bytes=60 * 1024 * 1024
         ),
-    )(heads, residual_in, norm_gain.reshape(1, model), out_weight, w_gate, w_up, w_down)
+    )(heads, residual_in, norm_gain, out_weight, w_gate, w_up, w_down)
 
 
 def solution(mesh):

time: 83.7 us -> 83.2 us (level)
    unnamed x9 -> x7, local copies, waits for them, and re-layouts: 1.9 us -> 1.9 us
where the time goes in v4:
time: 83.2 us; the launch traced here: 82.8 us
  Pallas kernels  73.5 us (88%)
  matrix products  4.4 us (5%)
  other arithmetic  2.63 us (3%)
  local copies, waits for them, and re-layouts  2.23 us (3%)
    pallas_call x1, Pallas kernels, local(): pl.pallas_call(functools.partial(layer_kernel, n), out_shape=jax.ShapeDty...  73.5 us
    unnamed x7, local copies, waits for them, and re-layouts  1.9 us
    dot_general x1, matrix products, attend(): jnp.einsum('rkgl,rlkd->rkgd', weights, values_all, preferred_element_type...  1.67 us

profile of v4, /device:TPU:0, one launch (start us, length us, event | category | flops | bytes accessed | tf_op | source)
XLA Modules:
  0.0 82.8 jit_solution(14626680168618225209)
XLA Ops:
  0.0 0.0 copy-start
  0.0 0.0 copy-start.2
  0.0 0.0 copy-start.1
  0.0 0.8 iota_compare_fusion.2
  0.8 0.4 copy-done
  1.2 1.6 %fusion.21 = (f32[8,4,16]{2,1,0:T(4,128)S(1)}, f32[8,4,16,128]{3,2,1,0:T(8,128)S(1)}) fusion(bf16[8,4,16,128]{3,0,2,1:T(8,128)(2,1)} %bitcast.37, pred[8,128]{1,0:T(8,128)(4,1)S(1)} %iota_compare_fusion.2, bf16[8,128,512]{2,1,0:T(8,128)(2,1)S(1)} %copy-done), kind=kOutput, calls=%fused_computation.37 | convolution fusion | flops 16973312 | bytes 1444864 | tf_op jit(solution)/shard_map/rkgd,rlkd->rkgl/dot_general | solution.py:26
  2.9 1.1 %fusion.13 = f32[8,4,1,16]{3,2,1,0:T(1,128)S(1)} fusion(bf16[8,4,16,128]{3,0,2,1:T(8,128)(2,1)} %bitcast.38, bf16[8,4,128,1]{2,0,1,3:T(8,128)(2,1)} %bitcast.42), kind=kOutput, calls=%fused_computation.19 | convolution fusion | flops 131072 | bytes 141312 | tf_op jit(solution)/shard_map/rkgd,rkd->rkg/dot_general | solution.py:30
  4.0 0.3 fusion.7
  4.3 0.7 bitcast_convert_fusion
  5.0 1.7 %fusion.1 = bf16[8,4,16,128]{3,2,1,0:T(8,128)(2,1)S(1)} fusion(f32[8,4,16,128]{3,2,1,0:T(8,128)S(1)} %get-tuple-element.10, f32[8,4,128]{2,1,0:T(4,128)S(1)} %copy.31, f32[8,4,16]{2,1,0:T(4,128)S(1)} %get-tuple-element.6, f32[8,4,16]{2,1,0:T(4,128)S(1)} %get-tuple-element.5, f32[8,4,16]{2,1,0:T(4,128)S(1)} %multiply_maximum_fusion, ...), kind=kOutput, calls=%fused_computation.3 | convolution fusion | flops 17235968 | bytes 1465344 | tf_op jit(solution)/shard_map/rkgl,rlkd->rkgd/dot_general | solution.py:46
  6.7 0.1 convert_element_type.36
  6.8 0.1 copy.57
  6.9 0.0 copy-done.2
  6.9 0.0 copy-done.1
  6.9 0.1 select_reduce_fusion
  7.0 0.1 copy.33
  7.2 0.7 fusion.8.refs_0_
  7.9 73.5 %shard_map.136 = bf16[8,4096]{1,0:T(8,128)(2,1)} custom-call(bf16[16,16,384]{2,1,0:T(8,128)(2,1)} %fusion.8.refs_0_, bf16[8,4096]{1,0:T(8,128)(2,1)} %refs_1_.1, bf16[4096]{0:T(1024)(128)(2,1)} %refs_2_.1, bf16[512,4096]{1,0:T(8,128)(2,1)} %refs_3_.1, bf16[1,4096,384]{2,1,0:T(8,128)(2,1)} %refs_4_.1, bf16[1,4096,384]{2,1,0:T(8,128)(2,1)} %refs_5_.1, ...), custom_call_target="tpu_custom_call" | custom-call | tf_op jit(solution)/shard_map/pallas_call | solution.py:397
  81.4 1.5 %copy.59 = bf16[8,4096]{1,0:T(8,128)(2,1)} copy(bf16[8,4096]{1,0:T(8,128)(2,1)} %shard_map.136) | data formatting | bytes 131072
  (5 shorter events, 0.1 us)
Async XLA Ops:
  0.0 1.2 %copy-start = (bf16[8,128,512]{2,1,0:T(8,128)(2,1)S(1)}, bf16[8,128,512]{2,1,0:T(8,128)(2,1)}, u32[]{:S(2)}) copy-start(bf16[8,128,512]{2,1,0:T(8,128)(2,1)} %param.16) | copy-start | bytes 3145732
  0.0 6.9 %copy-start.2 = (s32[8,8]{1,0:T(8,128)S(1)}, s32[8,8]{1,0:T(8,128)}, u32[]{:S(2)}) copy-start(s32[8,8]{1,0:T(8,128)} %param.23) | copy-start | bytes 772
  0.0 6.9 %copy-start.1 = (f32[8,8]{1,0:T(8,128)S(1)}, f32[8,8]{1,0:T(8,128)}, u32[]{:S(2)}) copy-start(f32[8,8]{1,0:T(8,128)} %param.24) | copy-start | bytes 772
